TPU v7x, 32 devices: a whole 2x2x4 slice. The times are simulated.
32 devices in a mesh: layer: 4 (over x, core), feat: 8 (over z, y).
Axes of the slice: x: 2, y: 2, z: 4, core: 2. Of those that a mesh axis runs over, the one named last changes fastest.
Arguments:
- inputs: bfloat16 [4, 512, 2304], P('layer', 'feat'), may hold values from -6 to 6
- targets: bfloat16 [4, 512, 2304], P('layer', 'feat'), may hold values from -64 to 64
- enc_weight: bfloat16 [4, 2304, 8192], P('layer', None, 'feat'), may hold values from -0.125 to 0.125
- enc_bias: float32 [4, 8192], P('layer', 'feat'), may hold values from -3 to 3
- dec_weight: bfloat16 [4, 4, 8192, 2304], P('layer', None, 'feat'), may hold values from -0.0625 to 0.0625
- dec_bias: float32 [4, 2304], P('layer'), may hold values from -3 to 3
Outputs:
- enc_grad: float32 [4, 2304, 8192], P('layer', None, 'feat')
- enc_bias_grad: float32 [4, 8192], P('layer', 'feat')
- dec_grad: float32 [4, 4, 8192, 2304], P('layer', None, 'feat')
- dec_bias_grad: float32 [4, 2304], P('layer')
- mean_square: float32 [], replicated
All inputs are finite; a program needn't handle non-finite values.
Results may differ from a plain program's by a relative error of at most 0.0095.
Values may be sent and summed in bfloat16 or wider, within the bound.
A program may use at most 192 MiB of HBM per device.

v0:
```python
import jax
import jax.numpy as jnp
from jax import lax
from jax.sharding import PartitionSpec as P

MB = 128


def body(inputs, targets, enc_weight, enc_bias, dec_weight, dec_bias):
    depth = dec_weight.shape[1]
    model_width = inputs.shape[2]
    layer_index = lax.axis_index("layer")
    gathered = lax.all_gather(inputs[0], "feat", axis=0, tiled=True)
    tok_count = gathered.shape[0]
    pre_act = jnp.dot(gathered, enc_weight[0], preferred_element_type=jnp.float32) + enc_bias[0]
    activity = jnp.maximum(pre_act, 0.0).astype(jnp.bfloat16)
    target_ids = jnp.arange(depth)
    valid_mask = (target_ids >= layer_index).astype(jnp.float32)
    partial_terms = jnp.einsum(
        "tf,mfd->mtd", activity, dec_weight[0], preferred_element_type=jnp.float32
    )
    partial_terms = partial_terms * valid_mask[:, None, None]
    rebuilt = lax.psum_scatter(
        partial_terms.reshape(depth * tok_count, model_width),
        ("layer", "feat"),
        scatter_dimension=0,
        tiled=True,
    )
    residual = rebuilt + dec_bias[0] - targets[0].astype(jnp.float32)
    squares = jnp.sum(residual * residual)
    bias_part = jnp.sum(residual, axis=0)
    bias_total = lax.psum(bias_part, "feat")
    square_total = lax.psum(squares, ("layer", "feat"))
    mean_square = square_total / (depth * tok_count * model_width)
    dec_bias_grad = (bias_total / MB)[None]
    residual_b = residual.astype(jnp.bfloat16)
    all_errors = lax.all_gather(residual_b, ("layer", "feat"), axis=0, tiled=True).reshape(
        depth, tok_count, model_width
    )
    every_kept = all_errors * valid_mask.astype(jnp.bfloat16)[:, None, None]
    dec_grad = (
        jnp.einsum("tf,mtd->mfd", activity, every_kept, preferred_element_type=jnp.float32) / MB
    )
    grad_act = (
        jnp.einsum("mtd,mfd->tf", every_kept, dec_weight[0], preferred_element_type=jnp.float32)
        / MB
    )
    grad_pre = jnp.where(pre_act > 0, grad_act, 0.0)
    enc_bias_grad = jnp.sum(grad_pre, axis=0)[None]
    enc_grad = jnp.dot(
        gathered.T, grad_pre.astype(jnp.bfloat16), preferred_element_type=jnp.float32
    )[None]
    return (enc_grad, enc_bias_grad, dec_grad[None], dec_bias_grad, mean_square)


def solution(mesh):
    placed = (
        P("layer", "feat", None),
        P("layer", "feat", None),
        P("layer", None, "feat"),
        P("layer", "feat"),
        P("layer", None, "feat", None),
        P("layer", None),
    )
    return jax.shard_map(
        body,
        mesh=mesh,
        in_specs=placed,
        out_specs=(
            P("layer", None, "feat"),
            P("layer", "feat"),
            P("layer", None, "feat", None),
            P("layer", None),
            P(),
        ),
        check_vma=False,
    )
```

profile of v0, /device:TPU:0, one launch (start us, length us, event | category | flops | bytes accessed | tf_op | source)
XLA Modules:
  0.0 490.1 jit_solution(18272403837166518245)
XLA Ops:
  7.2 0.0 all-gather.6.cloned.1.call-start
  7.2 0.7 all-gather.6.cloned.1.call-update
  7.9 0.0 reduce-scatter.2.cloned.1.call-start
  8.0 0.0 copy-start.3
  8.0 57.0 %all-gather.6.cloned.1.call-done = bf16[1,512,2304]{2,1,0:T(8,128)(2,1)} async-done(((bf16[1,64,2304]{2,1,0:T(8,128)(2,1)}), bf16[1,512,2304]{2,1,0:T(8,128)(2,1)}) %all-gather.6.cloned.1.call-update) | async-done | bytes 2359312 | tf_op jit(solution)/shard_map/all_gather | solution.py:13
  65.0 5.2 %fusion.9 = f32[512,1024]{1,0:T(8,128)S(1)} fusion(bf16[1,2304,1024]{2,1,0:T(8,128)(2,1)} %param.8, bf16[1,512,2304]{2,1,0:T(8,128)(2,1)} %all-gather.6.cloned.1.call-done), kind=kOutput, calls=%fused_computation.9 | convolution fusion | flops 2415919104 | bytes 9175040 | tf_op jit(solution)/shard_map/dot_general | solution.py:15
  70.2 0.0 copy-start.4
  70.2 0.0 copy-done.3
  70.2 18.3 %fusion.4 = f32[512,4,2304]{2,0,1:T(8,128)} fusion(bf16[1,4,1024,2304]{3,2,1,0:T(8,128)(2,1)} %param.10, f32[4]{0:T(128)S(1)} %compare_convert_fusion, f32[512,1024]{1,0:T(8,128)S(1)} %fusion.9, f32[1024]{0:T(1024)S(1)} %bitcast.53), kind=kOutput, calls=%fused_computation.5 | convolution fusion | flops 9669967872 | bytes 39850000 | tf_op jit(solution)/shard_map/tf,mfd->mtd/dot_general | solution.py:19
  88.5 0.0 copy-done.4
  88.5 0.0 copy-start.1
  88.5 0.0 copy-start
  88.5 0.0 reduce-scatter.2.cloned.1.call-update
  88.5 0.0 all-gather.4.cloned.1.call-start
  88.6 0.6 copy-done.1
  89.2 204.8 %reduce-scatter.2.cloned.1.call-done = f32[64,2304]{1,0:T(8,128)} async-done(((f32[2048,2304]{1,0:T(8,128)}), f32[64,2304]{1,0:T(8,128)}) %reduce-scatter.2.cloned.1.call-update) | async-done | bytes 589840 | tf_op jit(solution)/shard_map/reduce_scatter | solution.py:23
  294.0 0.0 copy-done
  294.0 2.5 multiply_reduce_fusion
  296.5 0.0 all-gather.4.cloned.1.call-update
  296.6 40.3 %psum.15 = f32[]{:T(128)} all-reduce(f32[]{:T(128)} %get-tuple-element.10), channel_id=1, replica_groups=mesh['layer'=4,'feat'=8] {'layer','feat'}, use_global_device_ids=true, to_apply=%region_5.6 | all-reduce | flops 1 | bytes 8 | tf_op jit(solution)/shard_map/psum | solution.py:33
  336.8 37.1 %psum.14 = f32[2304]{0:T(1024)S(1)} all-reduce(f32[2304]{0:T(1024)S(1)} %get-tuple-element.11), channel_id=1, replica_groups=mesh['layer'=4,'feat'=8] {'feat'}, use_global_device_ids=true, to_apply=%region_3.0 | all-reduce | flops 2304 | bytes 18432 | tf_op jit(solution)/shard_map/psum | solution.py:32
  374.0 0.6 broadcast_in_dim.19
  375.2 4.7 all-gather.4.cloned.1.call-done
  380.0 0.0 copy-start.5
  380.0 12.8 %copy.11 = bf16[4,512,2304]{1,2,0:T(8,128)(2,1)} copy(bf16[4,512,2304]{2,1,0:T(8,128)(2,1)} %bitcast.52) | data formatting | bytes 18874368 | tf_op jit(solution)/shard_map/reshape | solution.py:37
  392.7 0.0 copy-done.5
  392.7 17.6 %fusion.29 = (f32[1024]{0:T(1024)}, bf16[512,1024]{1,0:T(8,128)(2,1)S(1)}) fusion(bf16[1,4,1024,2304]{3,2,1,0:T(8,128)(2,1)} %param.10, bf16[4,512,2304]{1,2,0:T(8,128)(2,1)} %copy.11, bf16[4]{0:T(256)(128)(2,1)S(1)} %fusion.28, f32[512,1024]{1,0:T(8,128)S(1)} %copy-done.5, f32[1024]{0:T(1024)S(1)} %bitcast.54), kind=kOutput, calls=%fused_computation.29 | convolution fusion | flops 9671539712 | bytes 31465480 | tf_op jit(solution)/shard_map/mtd,mfd->tf/dot_general | solution.py:45
  410.3 0.0 copy-start.2
  410.3 20.6 %multiply_bitcast_fusion = f32[1,4,1024,2304]{2,3,1,0:T(8,128)} fusion(bf16[4,512,2304]{1,2,0:T(8,128)(2,1)} %copy.11, bf16[4]{0:T(256)(128)(2,1)S(1)} %fusion.28, f32[512,1024]{1,0:T(8,128)} %copy-done.4, f32[1024]{0:T(1024)S(1)} %bitcast.55), kind=kOutput, calls=%fused_computation | convolution fusion | flops 9679405056 | bytes 49287176 | tf_op jit(solution)/shard_map/tf,mtd->mfd/dot_general | solution.py:42
  430.9 0.0 copy-done.2
  430.9 5.2 %convolution_bitcast_fusion = f32[1,2304,1024]{1,2,0:T(8,128)} fusion(bf16[1,512,2304]{2,1,0:T(8,128)(2,1)S(1)} %copy-done.2, bf16[512,1024]{1,0:T(8,128)(2,1)S(1)} %get-tuple-element.14), kind=kOutput, calls=%fused_computation.8 | convolution fusion | flops 2415919104 | bytes 12845056 | tf_op jit(solution)/shard_map/dot_general | solution.py:50
  436.1 9.6 %copy.13 = f32[1,2304,1024]{2,1,0:T(8,128)} copy(f32[1,2304,1024]{1,2,0:T(8,128)} %convolution_bitcast_fusion) | data formatting | bytes 18874368
  445.7 36.8 %copy.14 = f32[1,4,1024,2304]{3,2,1,0:T(8,128)} copy(f32[1,4,1024,2304]{2,3,1,0:T(8,128)} %multiply_bitcast_fusion) | data formatting | bytes 75497472
  (4 shorter events, 0.0 us)
Async XLA Ops:
  7.2 57.8 %all-gather.6.cloned.1.call-start = ((), (), s32[]{:S(2)}) async-start(), calls=%async_computation.3 | async-start | bytes 2654208 | tf_op jit(solution)/shard_map/all_gather | solution.py:13
  7.9 286.1 %reduce-scatter.2.cloned.1.call-start = ((), (), s32[]{:S(2)}) async-start(), calls=%async_computation.1 | async-start | bytes 19464192 | tf_op jit(solution)/shard_map/reduce_scatter | solution.py:23
  8.0 62.2 %copy-start.3 = (f32[1,1024]{1,0:T(1,128)S(1)}, f32[1,1024]{1,0:T(1,128)}, u32[]{:S(2)}) copy-start(f32[1,1024]{1,0:T(1,128)} %param.9) | copy-start | bytes 12292
  70.2 18.3 %copy-start.4 = (f32[512,1024]{1,0:T(8,128)}, f32[512,1024]{1,0:T(8,128)S(1)}, u32[]{:S(2)}) copy-start(f32[512,1024]{1,0:T(8,128)S(1)} %fusion.9) | copy-start | bytes 6291460
  88.5 0.7 copy-start.1
  88.5 205.5 %copy-start = (bf16[1,64,2304]{2,1,0:T(8,128)(2,1)S(1)}, bf16[1,64,2304]{2,1,0:T(8,128)(2,1)}, u32[]{:S(2)}) copy-start(bf16[1,64,2304]{2,1,0:T(8,128)(2,1)} %param.7) | copy-start | bytes 884740
  88.5 291.4 %all-gather.4.cloned.1.call-start = ((), (), s32[]{:S(2)}) async-start(), calls=%async_computation.2 | async-start | bytes 9732096 | tf_op jit(solution)/shard_map/all_gather | solution.py:37
  380.0 12.8 %copy-start.5 = (f32[512,1024]{1,0:T(8,128)S(1)}, f32[512,1024]{1,0:T(8,128)}, u32[]{:S(2)}) copy-start(f32[512,1024]{1,0:T(8,128)} %copy-done.4) | copy-start | bytes 6291460
  410.3 20.6 %copy-start.2 = (bf16[1,512,2304]{2,1,0:T(8,128)(2,1)S(1)}, bf16[1,512,2304]{2,1,0:T(8,128)(2,1)}, u32[]{:S(2)}) copy-start(bf16[1,512,2304]{2,1,0:T(8,128)(2,1)} %all-gather.6.cloned.1.call-done) | copy-start | bytes 7077892
Sparse Core Ops, SparseCore 0:
  10.2 54.7 all-gather.5
  88.7 205.3 reduce-scatter.1
  297.5 82.3 all-gather.3
where the time goes:
time: 491 us; the launch traced here: 490 us
  waiting for transfers between devices  267 us (54%)
  blocking collectives  77.4 us (16%)
  matrix products  66.8 us (14%)
  local copies, waits for them, and re-layouts  60.4 us (12%)
  between operations  15.6 us (3%)
    reduce_scatter x1, waiting for transfers between devices, body(): lax.psum_scatter(partial_terms.reshape(depth * tok_count, model_width), (...  205 us
    all_gather x1, waiting for transfers between devices, body(): gathered = lax.all_gather(inputs[0], 'feat', axis=0, tiled=True)  57 us
    unnamed x14, local copies, waits for them, and re-layouts  47 us
    psum x1, blocking collectives, body(): square_total = lax.psum(squares, ('layer', 'feat'))  40.3 us
    psum x1, blocking collectives, body(): bias_total = lax.psum(bias_part, 'feat')  37.1 us
    dot_general x1, matrix products, body(): jnp.einsum('tf,mtd->mfd', activity, every_kept, preferred_element_type=jn...  20.6 us
    dot_general x1, matrix products, body(): jnp.einsum('tf,mfd->mtd', activity, dec_weight[0], preferred_element_type...  18.3 us
    dot_general x1, matrix products, body(): jnp.einsum('mtd,mfd->tf', every_kept, dec_weight[0], preferred_element_ty...  17.6 us
  transfers between devices with their start and end apart: 3, of which 3 were waited for; matrix products, arithmetic and copies ran while one was open for 0% of the time, Pallas kernels for 0%

commit v1 on v0

v1 whole, which is shorter than its diff:
```python
import functools

import jax
import jax.numpy as jnp
from jax import lax
from jax.experimental import pallas as pl
from jax.experimental.pallas import tpu as pltpu
from jax.sharding import PartitionSpec as P

MB = 128
MESH = pl.DeviceIdType.MESH
VMEM_BYTES = 60 * 1024 * 1024
ROW_TILE = 16


def bits_of(size):
    return size.bit_length() - 1


def flip(index, bit):
    own = (index // (1 << bit)) % 2
    return index + (1 - 2 * own) * (1 << bit), own


def flip_all(index, mask):
    bit = 0
    while mask >> bit:
        if (mask >> bit) & 1:
            index = flip(index, bit)[0]
        bit += 1
    return index


def enter(partners):
    barrier = pltpu.get_barrier_semaphore()
    for partner in partners:
        pl.semaphore_signal(barrier, inc=1, device_id=partner, device_id_type=MESH)
    pl.semaphore_wait(barrier, len(partners))


def gather_orders(n_bits):
    first = list(range(n_bits - 1, -1, -1))
    if n_bits < 2:
        return [first, first]
    second = first[:-2] + [first[-1], first[-2]]
    return [first, second]


def gather_kernel(n_bits, x_ref, out_ref, buf, local_sem, out_sem, send_sem, recv_sem):
    layer = lax.axis_index("layer")
    feat = lax.axis_index("feat")
    rows, width = x_ref.shape
    half = width // 2
    enter([(layer, flip(feat, b)[0]) for b in range(n_bits)])
    own_rows = pl.ds(pl.multiple_of(feat * rows, rows), rows)
    own = pltpu.make_async_copy(x_ref, buf.at[own_rows], local_sem)
    own.start()
    own.wait()
    orders = gather_orders(n_bits)

    def copy(j, slot, mask, bit):
        block = flip_all(feat, mask)
        at = buf.at[
            pl.ds(pl.multiple_of(block * rows, rows), rows), pl.ds(j * half, half)
        ]
        return pltpu.make_async_remote_copy(
            src_ref=at,
            dst_ref=at,
            send_sem=send_sem.at[j, slot],
            recv_sem=recv_sem.at[j, slot],
            device_id=(layer, flip(feat, bit)[0]),
            device_id_type=MESH,
        )

    all_copies = []
    held = [[0], [0]]
    sent = [{}, {}]
    for step in range(n_bits):
        for i in range(1 << step):
            for j in range(2):
                bit = orders[j][step]
                made = copy(j, (1 << step) - 1 + i, held[j][i], bit)
                made.start()
                all_copies.append(made)
                sent[j][step, i] = made
        for i in range(1 << step):
            for j in range(2):
                sent[j][step, i].wait_recv()
        for j in range(2):
            held[j] = held[j] + [m ^ (1 << orders[j][step]) for m in held[j]]
    for made in all_copies:
        made.wait_send()
    done = pltpu.make_async_copy(buf, out_ref, out_sem)
    done.start()
    done.wait()


def gather_tokens(block, feat_size):
    rows, width = block.shape
    n_bits = bits_of(feat_size)
    return pl.pallas_call(
        functools.partial(gather_kernel, n_bits),
        out_shape=jax.ShapeDtypeStruct((rows * feat_size, width), block.dtype),
        in_specs=[pl.BlockSpec(memory_space=pl.ANY)],
        out_specs=pl.BlockSpec(memory_space=pl.ANY),
        scratch_shapes=[
            pltpu.VMEM((rows * feat_size, width), block.dtype),
            pltpu.SemaphoreType.DMA,
            pltpu.SemaphoreType.DMA,
            pltpu.SemaphoreType.DMA((2, feat_size)),
            pltpu.SemaphoreType.DMA((2, feat_size)),
        ],
        compiler_params=pltpu.CompilerParams(
            collective_id=0, has_side_effects=True, vmem_limit_bytes=VMEM_BYTES
        ),
        name="gather_tokens",
    )(block)


def forward_kernel(depth, tiles, x_ref, w_ref, b_ref, dec_ref, bias_ref, goal_ref, pre_ref, act_ref, part_ref):
    layer = lax.axis_index("layer")
    feat = lax.axis_index("feat")
    step = pl.program_id(0)

    @pl.when(step == 0)
    def _():
        pre = jnp.dot(x_ref[...], w_ref[0], preferred_element_type=jnp.float32) + b_ref[...]
        pre_ref[...] = pre
        act_ref[...] = jnp.maximum(pre, 0.0).astype(jnp.bfloat16)

    target = step // tiles

    @pl.when(target >= layer)
    def _():
        part = jnp.dot(act_ref[...], dec_ref[0, 0], preferred_element_type=jnp.float32)
        part_ref[...] = part.astype(jnp.bfloat16)

    @pl.when(target < layer)
    def _():
        part_ref[...] = jnp.zeros_like(part_ref)

    @pl.when(target == layer)
    def _():
        rows = goal_ref.shape[1]
        mine = pl.ds(pl.multiple_of(feat * rows, rows), rows)
        shift = bias_ref[...] - goal_ref[0].astype(jnp.float32)
        part_ref[mine, :] = (part_ref[mine, :].astype(jnp.float32) + shift).astype(jnp.bfloat16)


def tile_of(width):
    for parts in (3, 2):
        if width % (128 * parts) == 0:
            return width // parts
    return width


def forward(gathered, enc_weight, enc_bias, dec_weight, dec_bias, targets):
    tok_count, width = gathered.shape
    feats = enc_weight.shape[2]
    depth = dec_weight.shape[1]
    tile = tile_of(width)
    tiles = width // tile
    rows = targets.shape[1]
    steps = depth * tiles
    return pl.pallas_call(
        functools.partial(forward_kernel, depth, tiles),
        grid=(steps,),
        out_shape=(
            jax.ShapeDtypeStruct((tok_count, feats), jnp.float32),
            jax.ShapeDtypeStruct((tok_count, feats), jnp.bfloat16),
            jax.ShapeDtypeStruct((depth * tok_count, width), jnp.bfloat16),
        ),
        in_specs=[
            pl.BlockSpec((tok_count, width), lambda i: (0, 0)),
            pl.BlockSpec((1, width, feats), lambda i: (0, 0, 0)),
            pl.BlockSpec((1, feats), lambda i: (0, 0)),
            pl.BlockSpec((1, 1, feats, tile), lambda i: (0, i // tiles, 0, i % tiles)),
            pl.BlockSpec((1, tile), lambda i: (0, i % tiles)),
            pl.BlockSpec((1, rows, tile), lambda i: (0, 0, i % tiles)),
        ],
        out_specs=(
            pl.BlockSpec((tok_count, feats), lambda i: (0, 0)),
            pl.BlockSpec((tok_count, feats), lambda i: (0, 0)),
            pl.BlockSpec((tok_count, tile), lambda i: (i // tiles, i % tiles)),
        ),
        compiler_params=pltpu.CompilerParams(vmem_limit_bytes=VMEM_BYTES),
        name="encode_decode",
    )(gathered, enc_weight, enc_bias, dec_weight, dec_bias, targets)


def exchange_kernel(layer_bits, feat_bits, groups, part_ref, out_ref, acc, first, res, *rest):
    n_steps = layer_bits - 1 + feat_bits
    received = rest[:n_steps]
    send_sem, recv_sem, local_sem, out_sem = rest[n_steps:]
    layer = lax.axis_index("layer")
    feat = lax.axis_index("feat")
    total_rows, width = part_ref.shape
    rows = total_rows // groups
    half = width // 2
    cols = half // 3

    sibling, core = flip(layer, 0)
    dims = []
    for b in range(1, layer_bits):
        there, own = flip(layer, b)
        dims.append(((there, feat), own))
    for b in range(feat_bits):
        there, own = flip(feat, b)
        dims.append(((layer, there), own))
    lead = min(3, n_steps)
    orders = []
    for j in range(3):
        turned = [dims[(j + i) % lead] for i in range(lead)]
        orders.append(turned + dims[lead:])
    sibling = (sibling, feat)
    enter([sibling] + [d[0] for d in dims])

    offsets = []
    for j in range(3):
        at = [0]
        for k in range(n_steps):
            at.append(at[-1] + orders[j][k][1] * (rows >> (k + 1)))
        offsets.append(at)

    def span(g, start, size):
        return pl.ds(pl.multiple_of(g * rows + start, ROW_TILE), size)

    def lanes(side, j):
        return pl.ds(pl.multiple_of(side * half + j * cols, 128), cols)

    def local_lanes(j):
        return pl.ds(j * cols, cols)

    copies = []

    def send(g, j, slot, src, dst, partner):
        made = pltpu.make_async_remote_copy(
            src_ref=src,
            dst_ref=dst,
            send_sem=send_sem.at[g, j, slot],
            recv_sem=recv_sem.at[g, j, slot],
            device_id=partner,
            device_id_type=MESH,
        )
        made.start()
        copies.append(made)
        return made

    pending = {}

    def start_scatter(g, j, k):
        partner, own = orders[j][k]
        size = rows >> (k + 1)
        away = offsets[j][k] + (1 - own) * size
        pending[g, j] = send(
            g, j, 1 + k,
            acc.at[span(g, away, size), local_lanes(j)],
            received[k].at[pl.ds(g * size, size), local_lanes(j)],
            partner,
        )

    def start_gather(g, j, k):
        partner, _ = orders[j][k]
        size = rows >> (k + 1)
        at = res.at[span(g, offsets[j][k + 1], size), lanes(core, j)]
        pending[g, j] = send(g, j, 1 + n_steps + k, at, at, partner)

    def stage(g, j, s):
        if s == 0:
            local[g, j].wait()
            pending[g, j].wait_recv()
            at = (span(g, 0, rows), local_lanes(j))
            acc[at] = acc[at] + first[at]
            start_scatter(g, j, 0)
        elif s <= n_steps:
            k = s - 1
            pending[g, j].wait_recv()
            size = rows >> (k + 1)
            keep = span(g, offsets[j][k + 1], size)
            summed = acc[keep, local_lanes(j)] + received[k][pl.ds(g * size, size), local_lanes(j)]
            if k + 1 < n_steps:
                acc[keep, local_lanes(j)] = summed
                start_scatter(g, j, k + 1)
            else:
                res[keep, lanes(core, j)] = summed
                start_gather(g, j, k)
        elif s <= 2 * n_steps:
            k = 2 * n_steps - s
            pending[g, j].wait_recv()
            if k > 0:
                start_gather(g, j, k - 1)
            else:
                at = res.at[span(g, 0, rows), lanes(core, j)]
                pending[g, j] = send(g, j, 1 + 2 * n_steps, at, at, sibling)
        else:
            pending[g, j].wait_recv()

    local = {}
    for g in range(groups):
        for j in range(3):
            pending[g, j] = send(
                g, j, 0,
                part_ref.at[span(g, 0, rows), lanes(1 - core, j)],
                first.at[span(g, 0, rows), local_lanes(j)],
                sibling,
            )
            made = pltpu.make_async_copy(
                part_ref.at[span(g, 0, rows), lanes(core, j)],
                acc.at[span(g, 0, rows), local_lanes(j)],
                local_sem.at[g, j],
            )
            made.start()
            local[g, j] = made
    n_stages = 2 * n_steps + 2
    outs = []
    for wave in range(groups + n_stages - 1):
        for g in range(groups):
            s = wave - g
            if 0 <= s < n_stages:
                for j in range(3):
                    stage(g, j, s)
                if s == n_stages - 1:
                    made = pltpu.make_async_copy(
                        res.at[span(g, 0, rows)],
                        out_ref.at[span(g, 0, rows)],
                        out_sem.at[g],
                    )
                    made.start()
                    outs.append(made)
    for made in copies:
        made.wait_send()
    for made in outs:
        made.wait()


def exchange(parts, layer_size, feat_size, tok_count):
    total_rows, width = parts.shape
    layer_bits, feat_bits = bits_of(layer_size), bits_of(feat_size)
    n_steps = layer_bits - 1 + feat_bits
    rows = max(tok_count, ROW_TILE << n_steps)
    groups = total_rows // rows
    half = width // 2
    slots = 2 * n_steps + 2
    bf16 = jnp.bfloat16
    return pl.pallas_call(
        functools.partial(exchange_kernel, layer_bits, feat_bits, groups),
        out_shape=jax.ShapeDtypeStruct(parts.shape, bf16),
        in_specs=[pl.BlockSpec(memory_space=pl.ANY)],
        out_specs=pl.BlockSpec(memory_space=pl.ANY),
        scratch_shapes=[
            pltpu.VMEM((total_rows, half), bf16),
            pltpu.VMEM((total_rows, half), bf16),
            pltpu.VMEM((total_rows, width), bf16),
        ]
        + [pltpu.VMEM((total_rows >> (k + 1), half), bf16) for k in range(n_steps)]
        + [
            pltpu.SemaphoreType.DMA((groups, 3, slots)),
            pltpu.SemaphoreType.DMA((groups, 3, slots)),
            pltpu.SemaphoreType.DMA((groups, 3)),
            pltpu.SemaphoreType.DMA((groups,)),
        ],
        compiler_params=pltpu.CompilerParams(
            collective_id=1, has_side_effects=True, vmem_limit_bytes=VMEM_BYTES
        ),
        name="exchange_residual",
    )(parts)


def backward_kernel(
    depth, tiles, res_ref, dec_ref, act_ref, pre_ref, x_ref,
    dec_grad_ref, enc_grad_ref, enc_bias_ref, dec_bias_ref, square_ref,
    turned, grad_act, grad_pre, squares,
):
    layer = lax.axis_index("layer")
    step = pl.program_id(0)
    main = depth * tiles
    target = step // tiles
    scale = 1.0 / MB

    @pl.when(step == 0)
    def _():
        turned[...] = act_ref[...].T
        grad_act[...] = jnp.zeros_like(grad_act)
        squares[...] = jnp.zeros_like(squares)

    @pl.when(step < main)
    def _():
        wide = res_ref[...].astype(jnp.float32)
        squares[...] += jnp.sum((wide * wide).reshape(-1, 8, wide.shape[1]), axis=0)

        @pl.when(target == layer)
        def _():
            dec_bias_ref[0, pl.ds(step % tiles, 1), :] = jnp.sum(wide, axis=0, keepdims=True) * scale

    @pl.when((step < main) & (target >= layer))
    def _():
        dec_grad_ref[0, 0] = (
            jnp.dot(turned[...], res_ref[...], preferred_element_type=jnp.float32) * scale
        )
        grad_act[...] += lax.dot_general(
            res_ref[...], dec_ref[0, 0], (((1,), (1,)), ((), ())),
            preferred_element_type=jnp.float32,
        )

    @pl.when((step < main) & (target < layer))
    def _():
        dec_grad_ref[...] = jnp.zeros_like(dec_grad_ref)

    @pl.when(step == main - 1)
    def _():
        grad = jnp.where(pre_ref[...] > 0, grad_act[...] * scale, 0.0)
        enc_bias_ref[...] = jnp.sum(grad, axis=0, keepdims=True)
        grad_pre[...] = grad.astype(jnp.bfloat16)
        square_ref[...] = jnp.sum(squares[...], keepdims=True)

    @pl.when(step >= main)
    def _():
        enc_grad_ref[0] = lax.dot_general(
            x_ref[...], grad_pre[...], (((0,), (0,)), ((), ())),
            preferred_element_type=jnp.float32,
        )


def backward(res, dec_weight, act, pre, gathered):
    tok_count, width = gathered.shape
    feats = act.shape[1]
    depth = dec_weight.shape[1]
    tile = tile_of(width)
    tiles = width // tile
    main = depth * tiles

    def tile_at(i):
        return jnp.minimum(i, main - 1)

    def late(i):
        return jnp.maximum(i - main, 0)

    return pl.pallas_call(
        functools.partial(backward_kernel, depth, tiles),
        grid=(main + tiles,),
        out_shape=(
            jax.ShapeDtypeStruct((1, depth, feats, width), jnp.float32),
            jax.ShapeDtypeStruct((1, width, feats), jnp.float32),
            jax.ShapeDtypeStruct((1, feats), jnp.float32),
            jax.ShapeDtypeStruct((1, tiles, tile), jnp.float32),
            jax.ShapeDtypeStruct((1, 1), jnp.float32),
        ),
        in_specs=[
            pl.BlockSpec((tok_count, tile), lambda i: (tile_at(i) // tiles, tile_at(i) % tiles)),
            pl.BlockSpec(
                (1, 1, feats, tile), lambda i: (0, tile_at(i) // tiles, 0, tile_at(i) % tiles)
            ),
            pl.BlockSpec((tok_count, feats), lambda i: (0, 0)),
            pl.BlockSpec((tok_count, feats), lambda i: (0, 0)),
            pl.BlockSpec((tok_count, tile), lambda i: (0, late(i))),
        ],
        out_specs=(
            pl.BlockSpec(
                (1, 1, feats, tile), lambda i: (0, tile_at(i) // tiles, 0, tile_at(i) % tiles)
            ),
            pl.BlockSpec((1, tile, feats), lambda i: (0, late(i), 0)),
            pl.BlockSpec((1, feats), lambda i: (0, 0)),
            pl.BlockSpec((1, tiles, tile), lambda i: (0, 0, 0)),
            pl.BlockSpec((1, 1), lambda i: (0, 0)),
        ),
        scratch_shapes=[
            pltpu.VMEM((feats, tok_count), jnp.bfloat16),
            pltpu.VMEM((tok_count, feats), jnp.float32),
            pltpu.VMEM((tok_count, feats), jnp.bfloat16),
            pltpu.VMEM((8, tile), jnp.float32),
        ],
        compiler_params=pltpu.CompilerParams(vmem_limit_bytes=VMEM_BYTES),
        name="backward",
    )(res, dec_weight, act, pre, gathered)


def body(layer_size, feat_size, inputs, targets, enc_weight, enc_bias, dec_weight, dec_bias):
    depth = dec_weight.shape[1]
    gathered = gather_tokens(inputs[0], feat_size)
    tok_count, width = gathered.shape
    pre, act, parts = forward(gathered, enc_weight, enc_bias, dec_weight, dec_bias, targets)
    res = exchange(parts, layer_size, feat_size, tok_count)
    dec_grad, enc_grad, enc_bias_grad, dec_bias_grad, squares = backward(
        res, dec_weight, act, pre, gathered
    )
    mean_square = squares[0, 0] / (depth * tok_count * width)
    return enc_grad, enc_bias_grad, dec_grad, dec_bias_grad.reshape(1, width), mean_square


def solution(mesh):
    placed = (
        P("layer", "feat", None),
        P("layer", "feat", None),
        P("layer", None, "feat"),
        P("layer", "feat"),
        P("layer", None, "feat", None),
        P("layer", None),
    )
    return jax.shard_map(
        functools.partial(body, mesh.shape["layer"], mesh.shape["feat"]),
        mesh=mesh,
        in_specs=placed,
        out_specs=(
            P("layer", None, "feat"),
            P("layer", "feat"),
            P("layer", None, "feat", None),
            P("layer", None),
            P(),
        ),
        check_vma=False,
    )
```

time: 491 us -> 201 us (0.41)
  waiting for transfers between devices: 267 us -> 0 us
  Pallas kernels: 0 us -> 196 us
  blocking collectives: 77.4 us -> 0 us
  matrix products: 66.8 us -> 0 us
  local copies, waits for them, and re-layouts: 60.4 us -> 1.32 us
  between operations: 15.6 us -> 2.43 us
    reduce_scatter x1 -> x0, waiting for transfers between devices: 205 us -> none  [body(): lax.psum_scatter(partial_terms.reshape(depth * tok_count, model_width), (...]
    pallas_call x0 -> x4, Pallas kernels: none -> 196 us  [the longest x1 89.7 us: exchange(): pl.pallas_call(functools.partial(exchange_kernel, layer_bits, feat_bits,...]
    psum x2 -> x0, blocking collectives: 77.4 us -> none  [the longest x1 40.3 us: body(): square_total = lax.psum(squares, ('layer', 'feat'))]
    dot_general x5 -> x0, matrix products: 66.8 us -> none  [the longest x1 20.6 us: body(): jnp.einsum('tf,mtd->mfd', activity, every_kept, preferred_element_type=jn...]
    all_gather x2 -> x0, waiting for transfers between devices: 61.7 us -> none  [the longest x1 57 us: body(): gathered = lax.all_gather(inputs[0], 'feat', axis=0, tiled=True)]
    unnamed x14 -> x1, local copies, waits for them, and re-layouts: 47 us -> 1.32 us
    reshape x1 -> x0, local copies, waits for them, and re-layouts: 12.8 us -> none  [body(): lax.all_gather(residual_b, ('layer', 'feat'), axis=0, tiled=True)]
  transfers between devices with their start and end apart: 3 -> 0, of which waited for: 3 -> 0; matrix products, arithmetic and copies ran while one was open for 0% -> 0% of each run, Pallas kernels for 0% -> 0%
where the time goes in v1:
time: 201 us; the launch traced here: 200 us
  Pallas kernels  196 us (98%)
  between operations  2.43 us (1%)
    pallas_call x1, Pallas kernels, exchange(): pl.pallas_call(functools.partial(exchange_kernel, layer_bits, feat_bits,...  89.7 us
    pallas_call x1, Pallas kernels, gather_tokens(): pl.pallas_call(functools.partial(gather_kernel, n_bits), out_shape=jax.Sh...  42.7 us
    pallas_call x1, Pallas kernels, backward(): pl.pallas_call(functools.partial(backward_kernel, depth, tiles), grid=(ma...  39.2 us
    pallas_call x1, Pallas kernels, forward(): pl.pallas_call(functools.partial(forward_kernel, depth, tiles), grid=(ste...  24.5 us

profile of v1, /device:TPU:0, one launch (start us, length us, event | category | flops | bytes accessed | tf_op | source)
XLA Modules:
  0.0 199.9 jit_solution(12948268803348031330)
XLA Ops:
  0.6 42.7 %gather_tokens.1.x_ref = bf16[512,2304]{1,0:T(8,128)(2,1)} custom-call(bf16[64,2304]{1,0:T(8,128)(2,1)} %bitcast.4), custom_call_target="tpu_custom_call" | custom-call | tf_op jit(solution)/shard_map/gather_tokens/pallas_call | solution.py:101
  43.4 24.5 %encode_decode.1 = (f32[512,1024]{1,0:T(8,128)}, bf16[512,1024]{1,0:T(8,128)(2,1)}, bf16[2048,2304]{1,0:T(8,128)(2,1)}) custom-call(bf16[512,2304]{1,0:T(8,128)(2,1)} %gather_tokens.1.x_ref, bf16[1,2304,1024]{2,1,0:T(8,128)(2,1)} %w_ref.1, f32[1,1024]{1,0:T(1,128)} %b_ref.1, bf16[1,4,1024,2304]{3,2,1,0:T(8,128)(2,1)} %dec_ref.3, f32[1,2304]{1,0:T(1,128)} %bias_ref.1, ...), custom_call_target="tpu_custom_call" | custom-call | tf_op jit(solution)/shard_map/encode_decode/pallas_call | solution.py:165
  67.8 89.7 %exchange_residual.1.res_ref = bf16[2048,2304]{1,0:T(8,128)(2,1)} custom-call(bf16[2048,2304]{1,0:T(8,128)(2,1)} %get-tuple-element.13.part_ref), custom_call_target="tpu_custom_call" | custom-call | tf_op jit(solution)/shard_map/exchange_residual/pallas_call | solution.py:345
  157.6 39.2 %backward.1 = (f32[1,4,1024,2304]{3,2,1,0:T(8,128)}, f32[1,2304,1024]{2,1,0:T(8,128)}, f32[1,1024]{1,0:T(1,128)}, f32[1,3,768]{2,1,0:T(4,128)}, f32[1,1]{1,0:T(1,128)}) custom-call(bf16[2048,2304]{1,0:T(8,128)(2,1)} %exchange_residual.1.res_ref, bf16[1,4,1024,2304]{3,2,1,0:T(8,128)(2,1)} %dec_ref.3, bf16[512,1024]{1,0:T(8,128)(2,1)} %get-tuple-element.14.act_ref, ...), custom_call_target="tpu_custom_call" | custom-call | tf_op jit(solution)/shard_map/backward/pallas_call | solution.py:438
  197.5 1.3 copy.11

commit v2 on v1

--- a/solution.py
+++ b/solution.py
@@ -38,32 +38,33 @@
     pl.semaphore_wait(barrier, len(partners))
 
 
-def gather_orders(n_bits):
+def gather_orders(n_bits, parts):
     first = list(range(n_bits - 1, -1, -1))
     if n_bits < 2:
-        return [first, first]
+        return [first] * parts
     second = first[:-2] + [first[-1], first[-2]]
-    return [first, second]
-
-
-def gather_kernel(n_bits, x_ref, out_ref, buf, local_sem, out_sem, send_sem, recv_sem):
+    return [second if j % 3 == 1 else first for j in range(parts)]
+
+
+def gather_kernel(n_bits, parts, x_ref, out_ref, buf, local_sem, out_sem, send_sem, recv_sem):
     layer = lax.axis_index("layer")
     feat = lax.axis_index("feat")
     rows, width = x_ref.shape
-    half = width // 2
+    cols = width // parts
+    own = pltpu.make_async_copy(
+        x_ref, buf.at[pl.ds(pl.multiple_of(feat * rows, rows), rows)], local_sem
+    )
+    own.start()
     enter([(layer, flip(feat, b)[0]) for b in range(n_bits)])
-    own_rows = pl.ds(pl.multiple_of(feat * rows, rows), rows)
-    own = pltpu.make_async_copy(x_ref, buf.at[own_rows], local_sem)
-    own.start()
     own.wait()
-    orders = gather_orders(n_bits)
+    orders = gather_orders(n_bits, parts)
 
     def copy(j, slot, mask, bit):
         block = flip_all(feat, mask)
         at = buf.at[
-            pl.ds(pl.multiple_of(block * rows, rows), rows), pl.ds(j * half, half)
+            pl.ds(pl.multiple_of(block * rows, rows), rows), pl.ds(j * cols, cols)
         ]
-        return pltpu.make_async_remote_copy(
+        made = pltpu.make_async_remote_copy(
             src_ref=at,
             dst_ref=at,
             send_sem=send_sem.at[j, slot],
@@ -71,35 +72,39 @@
             device_id=(layer, flip(feat, bit)[0]),
             device_id_type=MESH,
         )
-
-    all_copies = []
-    held = [[0], [0]]
-    sent = [{}, {}]
+        made.start()
+        return made
+
+    copies = []
+    held = [[0] for _ in range(parts)]
+    arriving = [[] for _ in range(parts)]
     for step in range(n_bits):
-        for i in range(1 << step):
-            for j in range(2):
-                bit = orders[j][step]
-                made = copy(j, (1 << step) - 1 + i, held[j][i], bit)
-                made.start()
-                all_copies.append(made)
-                sent[j][step, i] = made
-        for i in range(1 << step):
-            for j in range(2):
-                sent[j][step, i].wait_recv()
-        for j in range(2):
-            held[j] = held[j] + [m ^ (1 << orders[j][step]) for m in held[j]]
-    for made in all_copies:
-        made.wait_send()
+        for j in range(parts):
+            bit = orders[j][step]
+            started = []
+            for i, mask in enumerate(held[j]):
+                if i >= len(held[j]) - len(arriving[j]):
+                    arriving[j][i - len(held[j]) + len(arriving[j])].wait_recv()
+                started.append(copy(j, (1 << step) - 1 + i, mask, bit))
+            copies += started
+            arriving[j] = started
+            held[j] = held[j] + [m ^ (1 << bit) for m in held[j]]
+    for j in range(parts):
+        for made in arriving[j]:
+            made.wait_recv()
     done = pltpu.make_async_copy(buf, out_ref, out_sem)
     done.start()
+    for made in copies:
+        made.wait_send()
     done.wait()
 
 
 def gather_tokens(block, feat_size):
     rows, width = block.shape
     n_bits = bits_of(feat_size)
+    parts = next(p for p in (6, 3, 2, 1) if width % (128 * p) == 0)
     return pl.pallas_call(
-        functools.partial(gather_kernel, n_bits),
+        functools.partial(gather_kernel, n_bits, parts),
         out_shape=jax.ShapeDtypeStruct((rows * feat_size, width), block.dtype),
         in_specs=[pl.BlockSpec(memory_space=pl.ANY)],
         out_specs=pl.BlockSpec(memory_space=pl.ANY),
@@ -107,8 +112,8 @@
             pltpu.VMEM((rows * feat_size, width), block.dtype),
             pltpu.SemaphoreType.DMA,
             pltpu.SemaphoreType.DMA,
-            pltpu.SemaphoreType.DMA((2, feat_size)),
-            pltpu.SemaphoreType.DMA((2, feat_size)),
+            pltpu.SemaphoreType.DMA((parts, feat_size)),
+            pltpu.SemaphoreType.DMA((parts, feat_size)),
         ],
         compiler_params=pltpu.CompilerParams(
             collective_id=0, has_side_effects=True, vmem_limit_bytes=VMEM_BYTES

time: 201 us -> 196 us (0.975)
  Pallas kernels: 196 us -> 191 us
    pallas_call x1, Pallas kernels: 89.7 us -> 86.7 us  [exchange(): pl.pallas_call(functools.partial(exchange_kernel, layer_bits, feat_bits,...]
    pallas_call x1, Pallas kernels: 42.7 us -> 40.7 us  [gather_tokens(): pl.pallas_call(functools.partial(gather_kernel, n_bits, parts), out_shape...]
where the time goes in v2:
time: 196 us; the launch traced here: 195 us
  Pallas kernels  191 us (97%)
  between operations  2.43 us (1%)
    pallas_call x1, Pallas kernels, exchange(): pl.pallas_call(functools.partial(exchange_kernel, layer_bits, feat_bits,...  86.7 us
    pallas_call x1, Pallas kernels, gather_tokens(): pl.pallas_call(functools.partial(gather_kernel, n_bits, parts), out_shape...  40.7 us
    pallas_call x1, Pallas kernels, backward(): pl.pallas_call(functools.partial(backward_kernel, depth, tiles), grid=(ma...  39.2 us
    pallas_call x1, Pallas kernels, forward(): pl.pallas_call(functools.partial(forward_kernel, depth, tiles), grid=(ste...  24.5 us

profile of v2, /device:TPU:0, one launch (start us, length us, event | category | flops | bytes accessed | tf_op | source)
XLA Modules:
  0.0 194.8 jit_solution(6498188829680096089)
XLA Ops:
  0.6 40.7 %gather_tokens.1.x_ref = bf16[512,2304]{1,0:T(8,128)(2,1)} custom-call(bf16[64,2304]{1,0:T(8,128)(2,1)} %bitcast.4), custom_call_target="tpu_custom_call" | custom-call | tf_op jit(solution)/shard_map/gather_tokens/pallas_call | solution.py:106
  41.3 24.5 %encode_decode.1 = (f32[512,1024]{1,0:T(8,128)}, bf16[512,1024]{1,0:T(8,128)(2,1)}, bf16[2048,2304]{1,0:T(8,128)(2,1)}) custom-call(bf16[512,2304]{1,0:T(8,128)(2,1)} %gather_tokens.1.x_ref, bf16[1,2304,1024]{2,1,0:T(8,128)(2,1)} %w_ref.1, f32[1,1024]{1,0:T(1,128)} %b_ref.1, bf16[1,4,1024,2304]{3,2,1,0:T(8,128)(2,1)} %dec_ref.3, f32[1,2304]{1,0:T(1,128)} %bias_ref.1, ...), custom_call_target="tpu_custom_call" | custom-call | tf_op jit(solution)/shard_map/encode_decode/pallas_call | solution.py:170
  65.8 86.7 %exchange_residual.1.res_ref = bf16[2048,2304]{1,0:T(8,128)(2,1)} custom-call(bf16[2048,2304]{1,0:T(8,128)(2,1)} %get-tuple-element.13.part_ref), custom_call_target="tpu_custom_call" | custom-call | tf_op jit(solution)/shard_map/exchange_residual/pallas_call | solution.py:350
  152.5 39.2 %backward.1 = (f32[1,4,1024,2304]{3,2,1,0:T(8,128)}, f32[1,2304,1024]{2,1,0:T(8,128)}, f32[1,1024]{1,0:T(1,128)}, f32[1,3,768]{2,1,0:T(4,128)}, f32[1,1]{1,0:T(1,128)}) custom-call(bf16[2048,2304]{1,0:T(8,128)(2,1)} %exchange_residual.1.res_ref, bf16[1,4,1024,2304]{3,2,1,0:T(8,128)(2,1)} %dec_ref.3, bf16[512,1024]{1,0:T(8,128)(2,1)} %get-tuple-element.14.act_ref, ...), custom_call_target="tpu_custom_call" | custom-call | tf_op jit(solution)/shard_map/backward/pallas_call | solution.py:443
  192.4 1.3 copy.11

commit v3 on v2

--- a/solution.py
+++ b/solution.py
@@ -319,9 +319,13 @@
     n_stages = 2 * n_steps + 2
     outs = []
     for wave in range(groups + n_stages - 1):
+        for g in (0, 1) if wave == 0 else (wave + 1,):
+            if g < groups:
+                for j in range(3):
+                    stage(g, j, 0)
         for g in range(groups):
             s = wave - g
-            if 0 <= s < n_stages:
+            if 1 <= s < n_stages:
                 for j in range(3):
                     stage(g, j, s)
                 if s == n_stages - 1:

time: 196 us -> 194 us (0.990)
  Pallas kernels: 191 us -> 189 us
    pallas_call x1, Pallas kernels: 86.7 us -> 84.5 us  [exchange(): pl.pallas_call(functools.partial(exchange_kernel, layer_bits, feat_bits,...]
where the time goes in v3:
time: 194 us; the launch traced here: 193 us
  Pallas kernels  189 us (97%)
  between operations  2.43 us (1%)
    pallas_call x1, Pallas kernels, exchange(): pl.pallas_call(functools.partial(exchange_kernel, layer_bits, feat_bits,...  84.5 us
    pallas_call x1, Pallas kernels, gather_tokens(): pl.pallas_call(functools.partial(gather_kernel, n_bits, parts), out_shape...  40.7 us
    pallas_call x1, Pallas kernels, backward(): pl.pallas_call(functools.partial(backward_kernel, depth, tiles), grid=(ma...  39.2 us
    pallas_call x1, Pallas kernels, forward(): pl.pallas_call(functools.partial(forward_kernel, depth, tiles), grid=(ste...  24.5 us

profile of v3, /device:TPU:0, one launch (start us, length us, event | category | flops | bytes accessed | tf_op | source)
XLA Modules:
  0.0 192.7 jit_solution(4569914564635602005)
XLA Ops:
  0.6 40.7 %gather_tokens.1.x_ref = bf16[512,2304]{1,0:T(8,128)(2,1)} custom-call(bf16[64,2304]{1,0:T(8,128)(2,1)} %bitcast.4), custom_call_target="tpu_custom_call" | custom-call | tf_op jit(solution)/shard_map/gather_tokens/pallas_call | solution.py:106
  41.3 24.5 %encode_decode.1 = (f32[512,1024]{1,0:T(8,128)}, bf16[512,1024]{1,0:T(8,128)(2,1)}, bf16[2048,2304]{1,0:T(8,128)(2,1)}) custom-call(bf16[512,2304]{1,0:T(8,128)(2,1)} %gather_tokens.1.x_ref, bf16[1,2304,1024]{2,1,0:T(8,128)(2,1)} %w_ref.1, f32[1,1024]{1,0:T(1,128)} %b_ref.1, bf16[1,4,1024,2304]{3,2,1,0:T(8,128)(2,1)} %dec_ref.3, f32[1,2304]{1,0:T(1,128)} %bias_ref.1, ...), custom_call_target="tpu_custom_call" | custom-call | tf_op jit(solution)/shard_map/encode_decode/pallas_call | solution.py:170
  65.8 84.5 %exchange_residual.1.res_ref = bf16[2048,2304]{1,0:T(8,128)(2,1)} custom-call(bf16[2048,2304]{1,0:T(8,128)(2,1)} %get-tuple-element.13.part_ref), custom_call_target="tpu_custom_call" | custom-call | tf_op jit(solution)/shard_map/exchange_residual/pallas_call | solution.py:354
  150.3 39.2 %backward.1 = (f32[1,4,1024,2304]{3,2,1,0:T(8,128)}, f32[1,2304,1024]{2,1,0:T(8,128)}, f32[1,1024]{1,0:T(1,128)}, f32[1,3,768]{2,1,0:T(4,128)}, f32[1,1]{1,0:T(1,128)}) custom-call(bf16[2048,2304]{1,0:T(8,128)(2,1)} %exchange_residual.1.res_ref, bf16[1,4,1024,2304]{3,2,1,0:T(8,128)(2,1)} %dec_ref.3, bf16[512,1024]{1,0:T(8,128)(2,1)} %get-tuple-element.14.act_ref, ...), custom_call_target="tpu_custom_call" | custom-call | tf_op jit(solution)/shard_map/backward/pallas_call | solution.py:447
  190.2 1.3 copy.11
